TPU v7x, 32 devices: a whole 2x2x4 slice. The times are simulated.
32 devices in a mesh: grp: 2 (over y), sec: 4 (over z), term: 4 (over x, core).
Axes of the slice: x: 2, y: 2, z: 4, core: 2. Of those that a mesh axis runs over, the one named last changes fastest.
Arguments:
- trial_vectors: bfloat16 [2, 8, 4, 128, 128], P(None, ('grp', 'sec')), parts along dimension 1, may hold values from -30 to 30
- left_ops: bfloat16 [8, 8, 128, 128], P('term', ('grp', 'sec')), parts along dimension 1, may hold values from -2 to 2, as said below
- right_ops: bfloat16 [8, 8, 128, 128], P('term', ('grp', 'sec')), parts along dimension 1, may hold values from -2 to 2, as said below
- term_mask: int32 [8, 8], P('term', ('grp', 'sec')), parts along dimension 1, may hold values 0 or 1
Outputs:
- residual: bfloat16 [2, 8, 4, 128, 128], P(None, ('grp', 'sec'), 'term'), parts along dimension 1
- subspace: float32 [4, 2], P('grp'), parts along dimension 0
There are 2 independent parts, one for each index of `grp`. A program takes and returns all parts, laid end to end along the dimension named above; each array names one. Nothing has to cross between parts.
Inputs may be any that keep to these rules, and one draw needn't show every extreme that they name: `left_ops`: environment operator blocks. `right_ops`: environment operator blocks.
All inputs are finite; a program needn't handle non-finite values. No bound on the sum of `term_mask` on one device may be relied on, other than what follows from the above.
Results may differ from a plain program's by a relative error of at most 0.0052.
Values may be sent and summed in bfloat16 or wider, within the bound.
A program may use at most 64 MiB of HBM per device.

v0:
```python
import jax
import jax.numpy as jnp
from jax import lax
from jax.sharding import PartitionSpec as P


def local(trial_vectors, left_ops, right_ops, term_mask):
    left_mat = left_ops * term_mask[:, :, None, None].astype(jnp.bfloat16)

    def left_apply(left_op):
        return jnp.einsum(
            "aij,vabjc->vabic", left_op, trial_vectors, preferred_element_type=jnp.float32
        ).astype(jnp.bfloat16)

    blocks = lax.map(left_apply, left_mat)
    turned_partial = jnp.einsum(
        "kvabic,kbdc->vabid",
        lax.all_to_all(blocks, "sec", split_axis=3, concat_axis=2, tiled=True),
        right_ops,
        preferred_element_type=jnp.float32,
    )
    partial_value = lax.all_to_all(turned_partial, "sec", split_axis=1, concat_axis=2, tiled=True)
    sector_count = partial_value.shape[2]
    row_share = sector_count // lax.axis_size("term")
    row_start = lax.axis_index("term") * row_share
    summed = lax.psum(partial_value, "term")
    sigma_rows = lax.dynamic_slice_in_dim(summed, row_start, row_share, 2)
    vec_rows = lax.dynamic_slice_in_dim(trial_vectors, row_start, row_share, 2).astype(jnp.float32)
    cross_part = jnp.einsum(
        "vabic,wabic->vw", vec_rows, sigma_rows, precision=lax.Precision.HIGHEST
    )
    norm_part = jnp.sum(vec_rows * vec_rows, axis=(1, 2, 3, 4))
    cross_sum, norm_sum = lax.psum((cross_part, norm_part), ("sec", "term"))
    block_size = trial_vectors.shape[-1]
    cell_count = jnp.float32(sector_count * sector_count * block_size * block_size)
    subspace = cross_sum / cell_count
    norms = norm_sum / cell_count
    ritz_values = jnp.diagonal(subspace) / norms
    residual = (sigma_rows - ritz_values[:, None, None, None, None] * vec_rows).astype(jnp.bfloat16)
    return (residual, subspace)


def solution(mesh):
    placed = (
        P(None, ("grp", "sec"), None, None, None),
        P("term", ("grp", "sec"), None, None),
        P("term", ("grp", "sec"), None, None),
        P("term", ("grp", "sec")),
    )
    return jax.shard_map(
        local,
        mesh=mesh,
        in_specs=placed,
        out_specs=(P(None, ("grp", "sec"), "term", None, None), P("grp", None)),
        check_vma=False,
    )
```

profile of v0, /device:TPU:0, one launch (start us, length us, event | category | flops | bytes accessed | tf_op | source)
XLA Modules:
  0.0 123.5 jit_solution(16522695619806825217)
XLA Ops:
  7.2 0.0 copy-start
  7.2 0.0 copy-start.3
  7.2 0.0 all-reduce.3.cloned.1.call-start
  7.2 0.6 copy-done.3
  7.9 0.9 broadcast_multiply_fusion
  8.8 2.5 %while.10 = (s32[]{:T(128)}, bf16[2,2,1,4,128,128]{5,4,0,1,2,3:T(8,128)(2,1)S(1)}, bf16[2,1,128,128]{3,2,1,0:T(8,128)(2,1)S(1)}, bf16[2,1,4,128,128]{4,3,2,0,1:T(8,128)(2,1)}, s32[]{:T(128)}) while((s32[]{:T(128)}, bf16[2,2,1,4,128,128]{5,4,0,1,2,3:T(8,128)(2,1)S(1)}, bf16[2,1,128,128]{3,2,1,0:T(8,128)(2,1)S(1)}, ...), condition=%wide.region_1.2_spmd, body=%wide.region_0.1_spmd.sunk | while | flops 33685504 | bytes 1081413 | solution.py:15
  8.8 1.2 fusion.19
  10.0 1.2 fusion.19
  11.3 20.6 %all_to_all.21 = bf16[2,2,1,4,128,128]{5,4,0,1,2,3:T(8,128)(2,1)S(1)} all-to-all(bf16[2,2,1,4,128,128]{5,4,0,1,2,3:T(8,128)(2,1)S(1)} %get-tuple-element.24), channel_id=1, replica_groups=mesh['grp'=2,'sec'=4,'term'=4] {'sec'}, dimensions={3} | all-to-all | bytes 1048576 | tf_op jit(solution)/shard_map/all_to_all | solution.py:18
  31.9 0.0 copy-done
  31.9 0.3 convolution_bitcast_fusion
  32.2 16.7 %all_to_all.22 = f32[2,4,1,128,128]{4,3,0,2,1:T(8,128)} all-to-all(f32[2,4,1,128,128]{4,3,0,2,1:T(8,128)S(1)} %copy.19), channel_id=1, replica_groups=mesh['grp'=2,'sec'=4,'term'=4] {'sec'}, dimensions={1} | all-to-all | bytes 1048576 | tf_op jit(solution)/shard_map/all_to_all | solution.py:22
  48.9 0.0 all-reduce.3.cloned.1.call-update
  49.0 0.9 copy-done.2
  49.9 0.1 copy.21
  50.0 0.1 fusion.7
  50.1 31.2 %all-reduce.3.cloned.1.call-done = f32[2,1,4,128,128]{4,3,0,2,1:T(8,128)} async-done(((f32[2,1,4,128,128]{4,3,0,2,1:T(8,128)}), f32[2,1,4,128,128]{4,3,0,2,1:T(8,128)}) %all-reduce.3.cloned.1.call-update) | async-done | bytes 524304 | tf_op jit(solution)/shard_map/psum | solution.py:26
  81.4 0.9 dynamic-slice_bitcast_fusion
  82.3 0.1 copy.22
  82.4 0.7 convolution_bitcast_fusion.1
  83.1 31.3 %all-reduce = (f32[2,2]{1,0:T(2,128)S(1)}, f32[2]{0:T(128)S(1)}) all-reduce(f32[2,2]{1,0:T(2,128)S(1)} %convolution_bitcast_fusion.1, f32[2]{0:T(128)S(1)} %fusion.7), channel_id=1, replica_groups=mesh['grp'=2,'sec'=4,'term'=4] {'sec','term'}, use_global_device_ids=true, to_apply=%region_3.4 | all-reduce | flops 6 | bytes 48 | tf_op jit(solution)/shard_map/psum | solution.py:33
  114.4 0.6 gather_fusion
  115.1 0.0 copy-done.1
  115.1 1.6 %fusion.10 = bf16[2,1,1,128,128]{4,3,2,1,0:T(8,128)(2,1)} fusion(f32[2,1,4,128,128]{4,3,0,2,1:T(8,128)} %all-reduce.3.cloned.1.call-done, s32[]{:T(128)S(6)} %select_n.8, f32[2]{0:T(128)S(1)} %multiply_divide_fusion, bf16[2,1,4,128,128]{4,3,2,1,0:T(8,128)(2,1)S(1)} %bitcast.66), kind=kLoop, calls=%fused_computation.18 | loop fusion | flops 131072 | bytes 262156
  (11 shorter events, 0.2 us)
Async XLA Ops:
  7.2 24.7 %copy-start = (bf16[2,1,128,128]{3,2,1,0:T(8,128)(2,1)S(1)}, bf16[2,1,128,128]{3,2,1,0:T(8,128)(2,1)}, u32[]{:S(2)}) copy-start(bf16[2,1,128,128]{3,2,1,0:T(8,128)(2,1)} %param.8) | copy-start | bytes 196612
  7.2 0.7 copy-start.3
  7.2 74.2 %all-reduce.3.cloned.1.call-start = ((), (), s32[]{:S(2)}) async-start(), calls=%async_computation.2 | async-start | bytes 1048576 | tf_op jit(solution)/shard_map/psum | solution.py:26
  48.9 1.0 copy-start.2
  114.4 0.6 copy-start.1
Sparse Core Ops, SparseCore 0:
  49.1 32.2 all-reduce.2
where the time goes:
time: 124 us
  blocking collectives  68.7 us (55%)
  waiting for transfers between devices  31.2 us (25%)
  between operations  14.1 us (11%)
  local copies, waits for them, and re-layouts  3.47 us (3%)
  matrix products  3.27 us (3%)
  other arithmetic  2.7 us (2%)
    psum x1, blocking collectives, local(): cross_sum, norm_sum = lax.psum((cross_part, norm_part), ('sec', 'term'))  31.3 us
    psum x1, waiting for transfers between devices, local(): summed = lax.psum(partial_value, 'term')  31.2 us
    all_to_all x1, blocking collectives, local(): lax.all_to_all(blocks, 'sec', split_axis=3, concat_axis=2, tiled=True)  20.6 us
    all_to_all x1, blocking collectives, local(): lax.all_to_all(turned_partial, 'sec', split_axis=1, concat_axis=2, tiled=...  16.7 us
  transfers between devices with their start and end apart: 1, of which 1 were waited for; matrix products, arithmetic and copies ran while one was open for 0% of the time, Pallas kernels for 0%

commit v1 on v0

v1 whole, which is shorter than its diff:
```python
import functools

import jax
import jax.numpy as jnp
from jax import lax
from jax.experimental import pallas as pl
from jax.experimental.pallas import tpu as pltpu
from jax.sharding import PartitionSpec as P

MESH = pl.DeviceIdType.MESH
F32 = jnp.float32
BF16 = jnp.bfloat16


def each(count, body, first=0):
    if count - first <= 16:
        for index in range(first, count):
            body(index)
    else:
        lax.fori_loop(first, count, lambda index, carry: (body(index), carry)[1], 0)


def kernel(
    sectors, terms, x_hbm, l_hbm, r_hbm, mask_ref, out_ref, sub_ref,
    x_buf, l_buf, r_own, r_buf, t_buf, stat, stat_buf,
    in_sem, l_send, l_recv, r_send, r_recv, s_send, s_recv,
):
    vectors, share, size = x_buf.shape[0], x_buf.shape[1], x_buf.shape[2]
    ops = r_own.shape[0]
    sec, term = lax.axis_index("sec"), lax.axis_index("term")
    group = sectors * terms

    def peer(step):
        there = lax.rem(sec * terms + term + step, group)
        return {"sec": there // terms, "term": lax.rem(there, terms)}

    l_in = pltpu.make_async_copy(l_hbm.at[:, 0], l_buf.at[0], in_sem.at[0])
    r_in = pltpu.make_async_copy(r_hbm.at[:, 0], r_own, in_sem.at[1])
    x_in = pltpu.make_async_copy(
        x_hbm.at[:, 0, pl.ds(term * share, share)], x_buf, in_sem.at[2]
    )
    r_in.start()
    l_in.start()
    x_in.start()

    barrier = pltpu.get_barrier_semaphore()

    def greet(step):
        pl.semaphore_signal(barrier, inc=1, device_id=peer(step), device_id_type=MESH)

    each(group, greet, 1)

    l_in.wait()
    for k in range(ops):
        keep = mask_ref[k, 0].astype(F32)
        l_buf[0, k] = (l_buf[0, k].astype(F32) * keep).astype(BF16)
    r_in.wait()
    pl.semaphore_wait(barrier, group - 1)

    owner = sec // share
    r_slot = lax.rem(owner - term + terms, terms) * share + lax.rem(sec, share)

    def r_copy(step, slot):
        return pltpu.make_async_remote_copy(
            src_ref=r_own,
            dst_ref=r_buf.at[slot],
            send_sem=r_send.at[step],
            recv_sem=r_recv.at[slot],
            device_id={"sec": lax.rem(sec + step, sectors), "term": owner},
            device_id_type=MESH,
        )

    def l_copy(step):
        return pltpu.make_async_remote_copy(
            src_ref=l_buf.at[0],
            dst_ref=l_buf.at[step],
            send_sem=l_send.at[step],
            recv_sem=l_recv.at[step],
            device_id={"sec": sec, "term": lax.rem(term + step, terms)},
            device_id_type=MESH,
        )

    each(sectors, lambda step: r_copy(step, r_slot).start(), 1)
    each(terms, lambda step: l_copy(step).start(), 1)

    @pl.when(owner != term)
    def _():
        r_copy(0, r_slot).start()

    @pl.when(owner == term)
    def _():
        pltpu.make_async_copy(r_own, r_buf.at[r_slot], r_recv.at[r_slot]).start()

    x_in.wait()
    x_wide = jnp.concatenate(
        [x_buf[v, b] for b in range(share) for v in range(vectors)], axis=1
    )

    def left(step):
        part = jnp.dot(
            l_buf[step].reshape(ops * size, size), x_wide, preferred_element_type=F32
        ).astype(BF16)
        for b in range(share):
            for v in range(vectors):
                at = (b * vectors + v) * size
                for k in range(ops):
                    t_buf[step, b, v * size:(v + 1) * size, k * size:(k + 1) * size] = part[
                        k * size:(k + 1) * size, at:at + size
                    ]

    left(0)
    for step in range(1, terms):
        l_copy(step).wait_recv()
        left(step)

    stat_rows = [jnp.zeros((1, size), F32)] * 8
    sigmas = []
    for b in range(share):
        sigma = jnp.zeros((vectors * size, size), F32)
        for step in range(terms):
            slot = step * share + b
            r_copy(0, slot).wait_recv()
            right = jnp.concatenate([r_buf[slot, k] for k in range(ops)], axis=1)
            sigma += lax.dot_general(
                t_buf[step, b], right, (((1,), (1,)), ((), ())), preferred_element_type=F32
            )
        sigmas.append(sigma)
        xs = [x_buf[v, b].astype(F32) for v in range(vectors)]
        for v in range(vectors):
            for w in range(vectors):
                stat_rows[v * vectors + w] += jnp.sum(
                    xs[v] * sigma[w * size:(w + 1) * size], axis=0, keepdims=True
                )
            stat_rows[vectors * vectors + v] += jnp.sum(xs[v] * xs[v], axis=0, keepdims=True)
    stat[...] = jnp.concatenate(stat_rows, axis=0)

    me = sec * terms + term

    def s_copy(step):
        return pltpu.make_async_remote_copy(
            src_ref=stat,
            dst_ref=stat_buf.at[me],
            send_sem=s_send.at[step],
            recv_sem=s_recv.at[me],
            device_id=peer(step),
            device_id_type=MESH,
        )

    each(group, lambda step: s_copy(step).start(), 1)
    pltpu.make_async_copy(stat, stat_buf.at[me], s_recv.at[me]).start()

    def s_wait(slot):
        pltpu.make_async_copy(stat, stat_buf.at[slot], s_recv.at[slot]).wait()

    each(group, s_wait)
    total = jnp.sum(jnp.sum(stat_buf[...], axis=0), axis=1, keepdims=True)
    total = total / F32(sectors * sectors * size * size)
    for v in range(vectors):
        for w in range(vectors):
            sub_ref[v:v + 1, w:w + 1] = total[v * vectors + w:v * vectors + w + 1]
    for v in range(vectors):
        own = v * vectors + v
        norm = vectors * vectors + v
        ritz = total[own:own + 1] / total[norm:norm + 1]
        for b in range(share):
            out_ref[v, 0, b] = (
                sigmas[b][v * size:(v + 1) * size] - ritz * x_buf[v, b].astype(F32)
            ).astype(BF16)

    each(sectors, lambda step: r_copy(step, r_slot).wait_send(), 1)
    each(terms, lambda step: l_copy(step).wait_send(), 1)
    each(group, lambda step: s_copy(step).wait_send(), 1)

    @pl.when(owner != term)
    def _():
        r_copy(0, r_slot).wait_send()


def local(sectors, terms, trial_vectors, left_ops, right_ops, term_mask):
    vectors, _, columns, size, _ = trial_vectors.shape
    ops = left_ops.shape[0]
    share = columns // terms
    group = sectors * terms
    any_space = pl.BlockSpec(memory_space=pl.ANY)
    return pl.pallas_call(
        functools.partial(kernel, sectors, terms),
        out_shape=(
            jax.ShapeDtypeStruct((vectors, 1, share, size, size), BF16),
            jax.ShapeDtypeStruct((vectors, vectors), F32),
        ),
        in_specs=[any_space, any_space, any_space, pl.BlockSpec(memory_space=pltpu.SMEM)],
        out_specs=(
            pl.BlockSpec(memory_space=pltpu.VMEM),
            pl.BlockSpec(memory_space=pltpu.VMEM),
        ),
        scratch_shapes=[
            pltpu.VMEM((vectors, share, size, size), BF16),
            pltpu.VMEM((terms, ops, size, size), BF16),
            pltpu.VMEM((ops, size, size), BF16),
            pltpu.VMEM((terms * share, ops, size, size), BF16),
            pltpu.VMEM((terms, share, vectors * size, ops * size), BF16),
            pltpu.VMEM((8, size), F32),
            pltpu.VMEM((group, 8, size), F32),
            pltpu.SemaphoreType.DMA((3,)),
            pltpu.SemaphoreType.DMA((terms,)),
            pltpu.SemaphoreType.DMA((terms,)),
            pltpu.SemaphoreType.DMA((sectors,)),
            pltpu.SemaphoreType.DMA((terms * share,)),
            pltpu.SemaphoreType.DMA((group,)),
            pltpu.SemaphoreType.DMA((group,)),
        ],
        compiler_params=pltpu.CompilerParams(
            collective_id=0, has_side_effects=True, vmem_limit_bytes=32 * 1024 * 1024
        ),
    )(trial_vectors, left_ops, right_ops, term_mask)


def solution(mesh):
    placed = (
        P(None, ("grp", "sec"), None, None, None),
        P("term", ("grp", "sec"), None, None),
        P("term", ("grp", "sec"), None, None),
        P("term", ("grp", "sec")),
    )
    return jax.shard_map(
        functools.partial(local, mesh.shape["sec"], mesh.shape["term"]),
        mesh=mesh,
        in_specs=placed,
        out_specs=(P(None, ("grp", "sec"), "term", None, None), P("grp", None)),
        check_vma=False,
    )
```

time: 124 us -> 24.2 us (0.20)
  blocking collectives: 68.7 us -> 0 us
  waiting for transfers between devices: 31.2 us -> 0 us
  Pallas kernels: 0 us -> 18.7 us
  between operations: 14.1 us -> 0.64 us
  matrix products: 3.27 us -> 0 us
  other arithmetic: 2.7 us -> 0 us
    all_to_all x2 -> x0, blocking collectives: 37.3 us -> none  [the longest x1 20.6 us: local(): lax.all_to_all(blocks, 'sec', split_axis=3, concat_axis=2, tiled=True)]
    psum x1 -> x0, blocking collectives: 31.3 us -> none  [local(): cross_sum, norm_sum = lax.psum((cross_part, norm_part), ('sec', 'term'))]
    psum x1 -> x0, waiting for transfers between devices: 31.2 us -> none  [local(): summed = lax.psum(partial_value, 'term')]
    pallas_call x0 -> x1, Pallas kernels: none -> 18.7 us  [local(): pl.pallas_call(functools.partial(kernel, sectors, terms), out_shape=(jax....]
    dot_general x4 -> x0, matrix products: 3.27 us -> none  [the longest x2 2.33 us: left_apply(): jnp.einsum('aij,vabjc->vabic', left_op, trial_vectors, preferred_element_...]
    unnamed x8 -> x9, local copies, waits for them, and re-layouts: 1.56 us -> 4.56 us
    unnamed x1 -> x0, other arithmetic: 1.62 us -> none
  transfers between devices with their start and end apart: 1 -> 0, of which waited for: 1 -> 0; matrix products, arithmetic and copies ran while one was open for 0% -> 0% of each run, Pallas kernels for 0% -> 0%
where the time goes in v1:
time: 24.2 us; the launch traced here: 23.9 us
  Pallas kernels  18.7 us (77%)
  local copies, waits for them, and re-layouts  4.56 us (19%)
  between operations  0.64 us (3%)
    pallas_call x1, Pallas kernels, local(): pl.pallas_call(functools.partial(kernel, sectors, terms), out_shape=(jax....  18.7 us
    unnamed x9, local copies, waits for them, and re-layouts  4.56 us

profile of v1, /device:TPU:0, one launch (start us, length us, event | category | flops | bytes accessed | tf_op | source)
XLA Modules:
  0.0 23.9 jit_solution(7164617013775649531)
XLA Ops:
  0.6 0.7 %copy.6.mask_ref = s32[2,1]{1,0:T(2,128)S(1)} copy(s32[2,1]{0,1:T(1,128)} %param.7) | data formatting | bytes 16 | tf_op args[3]
  1.4 0.0 copy-start
  1.4 0.9 %copy-done = bf16[2,1,4,128,128]{4,3,2,1,0:T(8,128)(2,1)S(1)} copy-done((bf16[2,1,4,128,128]{4,3,2,1,0:T(8,128)(2,1)S(1)}, bf16[2,1,4,128,128]{4,3,2,1,0:T(8,128)(2,1)}, u32[]{:S(2)}) %copy-start) | copy-done | bytes 262168
  2.3 0.0 copy-start.1
  2.3 0.8 %copy-done.1 = bf16[2,1,128,128]{3,2,1,0:T(8,128)(2,1)S(1)} copy-done((bf16[2,1,128,128]{3,2,1,0:T(8,128)(2,1)S(1)}, bf16[2,1,128,128]{3,2,1,0:T(8,128)(2,1)}, u32[]{:S(2)}) %copy-start.1) | copy-done | bytes 65560
  3.2 0.0 copy-start.2
  3.2 0.8 %copy-done.2 = bf16[2,1,128,128]{3,2,1,0:T(8,128)(2,1)S(1)} copy-done((bf16[2,1,128,128]{3,2,1,0:T(8,128)(2,1)S(1)}, bf16[2,1,128,128]{3,2,1,0:T(8,128)(2,1)}, u32[]{:S(2)}) %copy-start.2) | copy-done | bytes 65560
  4.0 18.7 %shard_map.59 = (bf16[2,1,1,128,128]{4,3,2,1,0:T(8,128)(2,1)S(1)}, f32[2,2]{1,0:T(2,128)S(1)}) custom-call(bf16[2,1,4,128,128]{4,3,2,1,0:T(8,128)(2,1)S(1)} %copy-done, bf16[2,1,128,128]{3,2,1,0:T(8,128)(2,1)S(1)} %copy-done.1, bf16[2,1,128,128]{3,2,1,0:T(8,128)(2,1)S(1)} %copy-done.2, s32[2,1]{1,0:T(2,128)S(1)} %copy.6.mask_ref), custom_call_target="tpu_custom_call" | custom-call | tf_op jit(solution)/shard_map/pallas_call | solution.py:185
  22.7 0.6 %copy.9 = bf16[2,1,1,128,128]{4,3,2,1,0:T(8,128)(2,1)} copy(bf16[2,1,1,128,128]{4,3,2,1,0:T(8,128)(2,1)S(1)} %get-tuple-element.4) | data formatting | bytes 131072
  23.4 0.6 %copy.10 = f32[2,2]{1,0:T(2,128)} copy(f32[2,2]{1,0:T(2,128)S(1)} %get-tuple-element.5) | data formatting | bytes 32
Async XLA Ops:
  1.4 0.9 %copy-start = (bf16[2,1,4,128,128]{4,3,2,1,0:T(8,128)(2,1)S(1)}, bf16[2,1,4,128,128]{4,3,2,1,0:T(8,128)(2,1)}, u32[]{:S(2)}) copy-start(bf16[2,1,4,128,128]{4,3,2,1,0:T(8,128)(2,1)} %x_hbm.1) | copy-start | bytes 786436
  2.3 0.8 %copy-start.1 = (bf16[2,1,128,128]{3,2,1,0:T(8,128)(2,1)S(1)}, bf16[2,1,128,128]{3,2,1,0:T(8,128)(2,1)}, u32[]{:S(2)}) copy-start(bf16[2,1,128,128]{3,2,1,0:T(8,128)(2,1)} %l_hbm.1) | copy-start | bytes 196612
  3.2 0.8 %copy-start.2 = (bf16[2,1,128,128]{3,2,1,0:T(8,128)(2,1)S(1)}, bf16[2,1,128,128]{3,2,1,0:T(8,128)(2,1)}, u32[]{:S(2)}) copy-start(bf16[2,1,128,128]{3,2,1,0:T(8,128)(2,1)} %r_hbm.1) | copy-start | bytes 196612

commit v2 on v1

v2 whole, which is shorter than its diff:
```python
import functools

import jax
import jax.numpy as jnp
from jax import lax
from jax.experimental import pallas as pl
from jax.experimental.pallas import tpu as pltpu
from jax.sharding import PartitionSpec as P

MESH = pl.DeviceIdType.MESH
F32 = jnp.float32
BF16 = jnp.bfloat16


def each(count, body, first=0):
    if count - first <= 16:
        for index in range(first, count):
            body(index)
    else:
        lax.fori_loop(first, count, lambda index, carry: (body(index), carry)[1], 0)


def kernel(
    sectors, terms, x_hbm, l_hbm, r_hbm, mask_hbm, out_ref, sub_ref,
    mask_ref, x_buf, l_buf, r_buf, r_more, t_buf, stat_buf,
    in_sem, l_send, l_recv, up_send, down_send, r_recv, more_send, more_recv, s_send, s_recv,
):
    vectors, share, size = x_buf.shape[0], x_buf.shape[1], x_buf.shape[2]
    ops = r_buf.shape[1]
    sec, term = lax.axis_index("sec"), lax.axis_index("term")
    pair, side = lax.div(term, 2), lax.rem(term, 2)
    pairs = terms // 2
    group = sectors * terms
    me = sec * terms + term

    def peer(step):
        there = lax.rem(me + step, group)
        return {"sec": lax.div(there, terms), "term": lax.rem(there, terms)}

    mask_in = pltpu.make_async_copy(mask_hbm, mask_ref, in_sem.at[3])
    l_in = pltpu.make_async_copy(l_hbm.at[:, 0], l_buf.at[term], in_sem.at[0])
    r_in = pltpu.make_async_copy(r_hbm.at[:, 0], r_buf.at[sec], in_sem.at[1])
    x_in = pltpu.make_async_copy(
        x_hbm.at[:, 0, pl.ds(term * share, share)], x_buf, in_sem.at[2]
    )
    mask_in.start()
    l_in.start()
    r_in.start()
    x_in.start()

    barrier = pltpu.get_barrier_semaphore()

    def greet(step):
        pl.semaphore_signal(barrier, inc=1, device_id=peer(step), device_id_type=MESH)

    each(group, greet, 1)

    mask_in.wait()
    l_in.wait()
    for k in range(ops):
        keep = mask_ref[0, k].astype(F32)
        l_buf[term, k] = (l_buf[term, k].astype(F32) * keep).astype(BF16)
    r_in.wait()
    pl.semaphore_wait(barrier, group - 1)

    def up_copy(block):
        return pltpu.make_async_remote_copy(
            src_ref=r_buf.at[block],
            dst_ref=r_buf.at[block],
            send_sem=up_send.at[block],
            recv_sem=r_recv.at[block],
            device_id={"sec": sec + 1, "term": term},
            device_id_type=MESH,
        )

    def down_copy(block):
        return pltpu.make_async_remote_copy(
            src_ref=r_buf.at[block],
            dst_ref=r_buf.at[block],
            send_sem=down_send.at[block],
            recv_sem=r_recv.at[block],
            device_id={"sec": sec - 1, "term": term},
            device_id_type=MESH,
        )

    def more_copy(block):
        owner = lax.div(block, share)
        far = lax.rem(lax.div(owner, 2) - pair + pairs, pairs)
        other = lax.rem(lax.rem(owner, 2) + side, 2)
        slot = (2 * far + other - 1) * share + lax.rem(block, share)
        return pltpu.make_async_remote_copy(
            src_ref=r_buf.at[block],
            dst_ref=r_more.at[slot],
            send_sem=more_send.at[block],
            recv_sem=more_recv.at[slot],
            device_id={"sec": sec, "term": owner},
            device_id_type=MESH,
        )

    def source(relation):
        far, other = relation // 2, relation % 2
        there = lax.rem(pair - far + pairs, pairs)
        return 2 * there + (1 - side if other else side)

    def l_copy(block, far, other):
        return pltpu.make_async_remote_copy(
            src_ref=l_buf.at[block],
            dst_ref=l_buf.at[block],
            send_sem=l_send.at[2 * block + other],
            recv_sem=l_recv.at[block],
            device_id={
                "sec": sec,
                "term": 2 * lax.rem(pair + far, pairs) + (1 - side if other else side),
            },
            device_id_type=MESH,
        )

    def l_far(far):
        return pltpu.make_async_remote_copy(
            src_ref=l_buf.at[term],
            dst_ref=l_buf.at[term],
            send_sem=l_send.at[2 * terms + far],
            recv_sem=l_recv.at[term],
            device_id={"sec": sec, "term": 2 * lax.rem(pair + far, pairs) + side},
            device_id_type=MESH,
        )

    def walk(step, act):
        if step == 0:
            steps = ((sec, True, True),)
        else:
            steps = ((sec - step, True, False), (sec + step, False, True))
        for block, up, down in steps:
            @pl.when((block >= 0) & (block < sectors))
            def _():
                if step and act == "go":
                    up_copy(block).wait_recv()
                for on, edge, copy in (
                    (up, sec + 1 < sectors, up_copy),
                    (down, sec >= 1, down_copy),
                    (True, lax.div(block, share) != term, more_copy),
                ):
                    if on:
                        @pl.when(edge)
                        def _():
                            if act == "go":
                                copy(block).start()
                            else:
                                copy(block).wait_send()

    walk(0, "go")
    for far in range(1, pairs):
        l_far(far).start()
    l_copy(term, 0, 1).start()

    x_in.wait()
    x_wide = jnp.concatenate(
        [x_buf[v, b] for b in range(share) for v in range(vectors)], axis=1
    )

    def left(relation):
        part = jnp.dot(
            l_buf[source(relation)].reshape(ops * size, size), x_wide,
            preferred_element_type=F32,
        ).astype(BF16)
        for b in range(share):
            for v in range(vectors):
                at = (b * vectors + v) * size
                for k in range(ops):
                    t_buf[relation, b, v * size:(v + 1) * size, k * size:(k + 1) * size] = part[
                        k * size:(k + 1) * size, at:at + size
                    ]

    left(0)
    if sectors > 1:
        walk(1, "go")
    for far in range(1, pairs):
        block = source(2 * far)
        l_copy(block, 0, 1).wait_recv()
        l_copy(block, 0, 1).start()
    for step in range(2, sectors):
        walk(step, "go")
        if step == 2:
            for far in range(1, pairs):
                left(2 * far)
    l_copy(source(1), 0, 1).wait_recv()
    left(1)
    for far in range(1, pairs):
        l_copy(source(2 * far + 1), 0, 1).wait_recv()
        left(2 * far + 1)
        if sectors <= 2:
            left(2 * far)

    stat_rows = [jnp.zeros((1, size), F32)] * 8
    sigmas = []
    for b in range(share):
        sigma = jnp.zeros((vectors * size, size), F32)
        for relation in range(terms):
            if relation:
                ref = r_more.at[(relation - 1) * share + b]
                pltpu.make_async_copy(ref, ref, more_recv.at[(relation - 1) * share + b]).wait()
            else:
                ref = r_buf.at[term * share + b]
            right = jnp.concatenate([ref[k] for k in range(ops)], axis=1)
            sigma += lax.dot_general(
                t_buf[relation, b], right, (((1,), (1,)), ((), ())),
                preferred_element_type=F32,
            )
        sigmas.append(sigma)
        xs = [x_buf[v, b].astype(F32) for v in range(vectors)]
        for v in range(vectors):
            for w in range(vectors):
                stat_rows[v * vectors + w] += jnp.sum(
                    xs[v] * sigma[w * size:(w + 1) * size], axis=0, keepdims=True
                )
            stat_rows[vectors * vectors + v] += jnp.sum(xs[v] * xs[v], axis=0, keepdims=True)
    sums = jnp.sum(jnp.concatenate(stat_rows, axis=0), axis=1, keepdims=True)
    here = lax.broadcasted_iota(jnp.int32, (8, size), 0)
    lane = lax.broadcasted_iota(jnp.int32, (8, size), 1)
    stat_buf[me] = jnp.sum(jnp.where(here == lane, sums, 0.0), axis=0, keepdims=True)

    def s_copy(step):
        return pltpu.make_async_remote_copy(
            src_ref=stat_buf.at[me],
            dst_ref=stat_buf.at[me],
            send_sem=s_send,
            recv_sem=s_recv,
            device_id=peer(step),
            device_id_type=MESH,
        )

    each(group, lambda step: s_copy(step).start(), 1)
    others = stat_buf.at[pl.ds(0, group - 1)]
    pltpu.make_async_copy(others, others, s_recv).wait()
    total = jnp.sum(stat_buf[...], axis=0) / F32(sectors * sectors * size * size)
    for v in range(vectors):
        sub_ref[v:v + 1, :] = total[:, v * vectors:(v + 1) * vectors]
    for v in range(vectors):
        own = v * vectors + v
        norm = vectors * vectors + v
        ritz = total[:, own:own + 1] / total[:, norm:norm + 1]
        for b in range(share):
            out_ref[v, 0, b] = (
                sigmas[b][v * size:(v + 1) * size] - ritz * x_buf[v, b].astype(F32)
            ).astype(BF16)

    for step in range(sectors):
        walk(step, "end")
    for far in range(1, pairs):
        l_far(far).wait_send()
    for far in range(pairs):
        l_copy(source(2 * far), 0, 1).wait_send()
    pltpu.make_async_copy(others, others, s_send).wait()


def local(sectors, terms, trial_vectors, left_ops, right_ops, term_mask):
    vectors, _, columns, size, _ = trial_vectors.shape
    ops = left_ops.shape[0]
    share = columns // terms
    group = sectors * terms
    hbm = pl.BlockSpec(memory_space=pltpu.HBM)
    return pl.pallas_call(
        functools.partial(kernel, sectors, terms),
        out_shape=(
            jax.ShapeDtypeStruct((vectors, 1, share, size, size), BF16),
            jax.ShapeDtypeStruct((vectors, vectors), F32),
        ),
        in_specs=[hbm] * 4,
        out_specs=(
            pl.BlockSpec(memory_space=pltpu.VMEM),
            pl.BlockSpec(memory_space=pltpu.VMEM),
        ),
        scratch_shapes=[
            pltpu.SMEM((1, ops), jnp.int32),
            pltpu.VMEM((vectors, share, size, size), BF16),
            pltpu.VMEM((terms, ops, size, size), BF16),
            pltpu.VMEM((columns, ops, size, size), BF16),
            pltpu.VMEM(((terms - 1) * share, ops, size, size), BF16),
            pltpu.VMEM((terms, share, vectors * size, ops * size), BF16),
            pltpu.VMEM((group, 1, size), F32),
            pltpu.SemaphoreType.DMA((4,)),
            pltpu.SemaphoreType.DMA((2 * terms + terms // 2,)),
            pltpu.SemaphoreType.DMA((terms,)),
            pltpu.SemaphoreType.DMA((columns,)),
            pltpu.SemaphoreType.DMA((columns,)),
            pltpu.SemaphoreType.DMA((columns,)),
            pltpu.SemaphoreType.DMA((columns,)),
            pltpu.SemaphoreType.DMA(((terms - 1) * share,)),
            pltpu.SemaphoreType.DMA,
            pltpu.SemaphoreType.DMA,
        ],
        compiler_params=pltpu.CompilerParams(
            collective_id=0, has_side_effects=True, vmem_limit_bytes=64 * 1024 * 1024
        ),
    )(trial_vectors, left_ops, right_ops, term_mask.T)


def solution(mesh):
    placed = (
        P(None, ("grp", "sec"), None, None, None),
        P("term", ("grp", "sec"), None, None),
        P("term", ("grp", "sec"), None, None),
        P("term", ("grp", "sec")),
    )
    return jax.shard_map(
        functools.partial(local, mesh.shape["sec"], mesh.shape["term"]),
        mesh=mesh,
        in_specs=placed,
        out_specs=(P(None, ("grp", "sec"), "term", None, None), P("grp", None)),
        check_vma=False,
    )
```

time: 24.2 us -> 26.7 us (1.10)
  Pallas kernels: 18.7 us -> 23.8 us
  local copies, waits for them, and re-layouts: 4.56 us -> 2.04 us
    pallas_call x1, Pallas kernels: 18.7 us -> 23.8 us  [local(): pl.pallas_call(functools.partial(kernel, sectors, terms), out_shape=(jax....]
    unnamed x9 -> x4, local copies, waits for them, and re-layouts: 4.56 us -> 2.04 us
where the time goes in v2:
time: 26.7 us; the launch traced here: 26.5 us
  Pallas kernels  23.8 us (89%)
  local copies, waits for them, and re-layouts  2.04 us (8%)
  between operations  0.65 us (2%)
    pallas_call x1, Pallas kernels, local(): pl.pallas_call(functools.partial(kernel, sectors, terms), out_shape=(jax....  23.8 us
    unnamed x4, local copies, waits for them, and re-layouts  2.04 us

profile of v2, /device:TPU:0, one launch (start us, length us, event | category | flops | bytes accessed | tf_op | source)
XLA Modules:
  0.0 26.5 jit_solution(15437547428739330503)
XLA Ops:
  0.6 23.8 %shard_map.59 = (bf16[2,1,1,128,128]{4,3,2,1,0:T(8,128)(2,1)}, f32[2,2]{1,0:T(2,128)}) custom-call(bf16[2,1,4,128,128]{4,3,2,1,0:T(8,128)(2,1)} %x_hbm.1, bf16[2,1,128,128]{3,2,1,0:T(8,128)(2,1)} %l_hbm.1, bf16[2,1,128,128]{3,2,1,0:T(8,128)(2,1)} %r_hbm.1, s32[1,2]{1,0:T(1,128)} %bitcast.1), custom_call_target="tpu_custom_call" | custom-call | tf_op jit(solution)/shard_map/pallas_call | solution.py:262
  24.5 0.0 copy-start
  24.5 1.5 %copy.8 = bf16[2,1,1,128,128]{4,3,2,1,0:T(8,128)(2,1)} copy(bf16[2,1,1,128,128]{4,3,2,1,0:T(8,128)(2,1)} %get-tuple-element.4) | data formatting | bytes 131072
  26.0 0.0 copy-done
  26.0 0.6 %copy.9 = f32[2,2]{1,0:T(2,128)} copy(f32[2,2]{1,0:T(2,128)S(1)} %copy-done) | data formatting | bytes 32
Async XLA Ops:
  24.5 1.5 %copy-start = (f32[2,2]{1,0:T(2,128)S(1)}, f32[2,2]{1,0:T(2,128)}, u32[]{:S(2)}) copy-start(f32[2,2]{1,0:T(2,128)} %get-tuple-element.5) | copy-start | bytes 52

commit v3 on v1

--- a/solution.py
+++ b/solution.py
@@ -21,8 +21,8 @@
 
 
 def kernel(
-    sectors, terms, x_hbm, l_hbm, r_hbm, mask_ref, out_ref, sub_ref,
-    x_buf, l_buf, r_own, r_buf, t_buf, stat, stat_buf,
+    sectors, terms, x_hbm, l_hbm, r_hbm, mask_hbm, out_hbm, sub_hbm,
+    out_ref, sub_ref, mask_ref, x_buf, l_buf, r_own, r_buf, t_buf, stat_buf,
     in_sem, l_send, l_recv, r_send, r_recv, s_send, s_recv,
 ):
     vectors, share, size = x_buf.shape[0], x_buf.shape[1], x_buf.shape[2]
@@ -39,8 +39,10 @@
     x_in = pltpu.make_async_copy(
         x_hbm.at[:, 0, pl.ds(term * share, share)], x_buf, in_sem.at[2]
     )
+    mask_in = pltpu.make_async_copy(mask_hbm, mask_ref, in_sem.at[3])
+    mask_in.start()
+    l_in.start()
     r_in.start()
-    l_in.start()
     x_in.start()
 
     barrier = pltpu.get_barrier_semaphore()
@@ -50,9 +52,10 @@
 
     each(group, greet, 1)
 
+    mask_in.wait()
     l_in.wait()
     for k in range(ops):
-        keep = mask_ref[k, 0].astype(F32)
+        keep = mask_ref[0, k].astype(F32)
         l_buf[0, k] = (l_buf[0, k].astype(F32) * keep).astype(BF16)
     r_in.wait()
     pl.semaphore_wait(barrier, group - 1)
@@ -132,48 +135,67 @@
                     xs[v] * sigma[w * size:(w + 1) * size], axis=0, keepdims=True
                 )
             stat_rows[vectors * vectors + v] += jnp.sum(xs[v] * xs[v], axis=0, keepdims=True)
-    stat[...] = jnp.concatenate(stat_rows, axis=0)
-
     me = sec * terms + term
+    sums = jnp.sum(jnp.concatenate(stat_rows, axis=0), axis=1, keepdims=True)
+    here = lax.broadcasted_iota(jnp.int32, (8, size), 0)
+    lane = lax.broadcasted_iota(jnp.int32, (8, size), 1)
+    stat_buf[me] = jnp.sum(jnp.where(here == lane, sums, 0.0), axis=0, keepdims=True)
 
     def s_copy(step):
         return pltpu.make_async_remote_copy(
-            src_ref=stat,
+            src_ref=stat_buf.at[me],
             dst_ref=stat_buf.at[me],
-            send_sem=s_send.at[step],
-            recv_sem=s_recv.at[me],
+            send_sem=s_send,
+            recv_sem=s_recv,
             device_id=peer(step),
             device_id_type=MESH,
         )
 
     each(group, lambda step: s_copy(step).start(), 1)
-    pltpu.make_async_copy(stat, stat_buf.at[me], s_recv.at[me]).start()
-
-    def s_wait(slot):
-        pltpu.make_async_copy(stat, stat_buf.at[slot], s_recv.at[slot]).wait()
-
-    each(group, s_wait)
-    total = jnp.sum(jnp.sum(stat_buf[...], axis=0), axis=1, keepdims=True)
-    total = total / F32(sectors * sectors * size * size)
+    others = stat_buf.at[pl.ds(0, group - 1)]
+    pltpu.make_async_copy(others, others, s_recv).wait()
+    total = jnp.sum(stat_buf[...], axis=0) / F32(sectors * sectors * size * size)
     for v in range(vectors):
-        for w in range(vectors):
-            sub_ref[v:v + 1, w:w + 1] = total[v * vectors + w:v * vectors + w + 1]
+        sub_ref[v:v + 1, :] = total[:, v * vectors:(v + 1) * vectors]
+    sub_out = pltpu.make_async_copy(sub_ref, sub_hbm, in_sem.at[1])
+    sub_out.start()
     for v in range(vectors):
         own = v * vectors + v
         norm = vectors * vectors + v
-        ritz = total[own:own + 1] / total[norm:norm + 1]
+        ritz = total[:, own:own + 1] / total[:, norm:norm + 1]
         for b in range(share):
-            out_ref[v, 0, b] = (
+            out_ref[v, b] = (
                 sigmas[b][v * size:(v + 1) * size] - ritz * x_buf[v, b].astype(F32)
             ).astype(BF16)
 
+    out = pltpu.make_async_copy(out_ref, out_hbm.at[:, 0], in_sem.at[0])
+    out.start()
+
     each(sectors, lambda step: r_copy(step, r_slot).wait_send(), 1)
     each(terms, lambda step: l_copy(step).wait_send(), 1)
-    each(group, lambda step: s_copy(step).wait_send(), 1)
+    pltpu.make_async_copy(others, others, s_send).wait()
 
     @pl.when(owner != term)
     def _():
         r_copy(0, r_slot).wait_send()
+
+    sub_out.wait()
+    out.wait()
+
+
+def hand_on(res_in, sub_in, res_out, sub_out, res, sub, sem):
+    res_load = pltpu.make_async_copy(res_in, res, sem.at[0])
+    sub_load = pltpu.make_async_copy(sub_in, sub, sem.at[1])
+    res_store = pltpu.make_async_copy(res, res_out, sem.at[2])
+    sub_store = pltpu.make_async_copy(sub, sub_out, sem.at[3])
+    res_load.start()
+    sub_load.start()
+    res_load.wait()
+    res_store.start()
+    sub_load.wait()
+    sub_store.start()
+    res_store.wait()
+    sub_store.wait()
 
 
 def local(sectors, terms, trial_vectors, left_ops, right_ops, term_mask):
@@ -181,38 +203,50 @@
     ops = left_ops.shape[0]
     share = columns // terms
     group = sectors * terms
-    any_space = pl.BlockSpec(memory_space=pl.ANY)
-    return pl.pallas_call(
+    hbm = pl.BlockSpec(memory_space=pltpu.HBM)
+    made = (
+        jax.ShapeDtypeStruct((vectors, 1, share, size, size), BF16),
+        jax.ShapeDtypeStruct((vectors, vectors), F32),
+    )
+    results = pl.pallas_call(
         functools.partial(kernel, sectors, terms),
-        out_shape=(
-            jax.ShapeDtypeStruct((vectors, 1, share, size, size), BF16),
-            jax.ShapeDtypeStruct((vectors, vectors), F32),
-        ),
-        in_specs=[any_space, any_space, any_space, pl.BlockSpec(memory_space=pltpu.SMEM)],
-        out_specs=(
-            pl.BlockSpec(memory_space=pltpu.VMEM),
-            pl.BlockSpec(memory_space=pltpu.VMEM),
-        ),
+        out_shape=made,
+        in_specs=[hbm] * 4,
+        out_specs=(hbm, hbm),
         scratch_shapes=[
+            pltpu.VMEM((vectors, share, size, size), BF16),
+            pltpu.VMEM((vectors, vectors), F32),
+            pltpu.SMEM((1, ops), jnp.int32),
             pltpu.VMEM((vectors, share, size, size), BF16),
             pltpu.VMEM((terms, ops, size, size), BF16),
             pltpu.VMEM((ops, size, size), BF16),
             pltpu.VMEM((terms * share, ops, size, size), BF16),
             pltpu.VMEM((terms, share, vectors * size, ops * size), BF16),
-            pltpu.VMEM((8, size), F32),
-            pltpu.VMEM((group, 8, size), F32),
-            pltpu.SemaphoreType.DMA((3,)),
+            pltpu.VMEM((group, 1, size), F32),
+            pltpu.SemaphoreType.DMA((4,)),
             pltpu.SemaphoreType.DMA((terms,)),
             pltpu.SemaphoreType.DMA((terms,)),
             pltpu.SemaphoreType.DMA((sectors,)),
             pltpu.SemaphoreType.DMA((terms * share,)),
-            pltpu.SemaphoreType.DMA((group,)),
-            pltpu.SemaphoreType.DMA((group,)),
+            pltpu.SemaphoreType.DMA,
+            pltpu.SemaphoreType.DMA,
         ],
         compiler_params=pltpu.CompilerParams(
-            collective_id=0, has_side_effects=True, vmem_limit_bytes=32 * 1024 * 1024
+            collective_id=0, has_side_effects=True, vmem_limit_bytes=64 * 1024 * 1024
         ),
-    )(trial_vectors, left_ops, right_ops, term_mask)
+    )(trial_vectors, left_ops, right_ops, term_mask.T)
+    return pl.pallas_call(
+        hand_on,
+        out_shape=made,
+        in_specs=[hbm, hbm],
+        out_specs=(hbm, hbm),
+        scratch_shapes=[
+            pltpu.VMEM(made[0].shape, BF16),
+            pltpu.VMEM(made[1].shape, F32),
+            pltpu.SemaphoreType.DMA((4,)),
+        ],
+        compiler_params=pltpu.CompilerParams(vmem_limit_bytes=64 * 1024 * 1024),
+    )(*results)
 
 
 def solution(mesh):

time: 24.2 us -> 20.7 us (0.86)
  local copies, waits for them, and re-layouts: 4.56 us -> 0 us
  Pallas kernels: 18.7 us -> 19.9 us
    unnamed x9 -> x0, local copies, waits for them, and re-layouts: 4.56 us -> none
    pallas_call x1 -> x2, Pallas kernels: 18.7 us -> 19.9 us  [the longest x1 18.4 us: local(): pl.pallas_call(functools.partial(kernel, sectors, terms), out_shape=made,...]
where the time goes in v3:
time: 20.7 us; the launch traced here: 20.5 us
  Pallas kernels  19.9 us (96%)
  between operations  0.64 us (3%)
    pallas_call x1, Pallas kernels, local(): pl.pallas_call(functools.partial(kernel, sectors, terms), out_shape=made,...  18.4 us
    pallas_call x1, Pallas kernels, local(): pl.pallas_call(hand_on, out_shape=made, in_specs=[hbm, hbm], out_specs=(h...  1.51 us

profile of v3, /device:TPU:0, one launch (start us, length us, event | category | flops | bytes accessed | tf_op | source)
XLA Modules:
  0.0 20.5 jit_solution(17229973340274392049)
XLA Ops:
  0.6 18.4 %shard_map.59 = (bf16[2,1,1,128,128]{4,3,2,1,0:T(8,128)(2,1)}, f32[2,2]{1,0:T(2,128)}) custom-call(bf16[2,1,4,128,128]{4,3,2,1,0:T(8,128)(2,1)} %x_hbm.1, bf16[2,1,128,128]{3,2,1,0:T(8,128)(2,1)} %l_hbm.1, bf16[2,1,128,128]{3,2,1,0:T(8,128)(2,1)} %r_hbm.1, s32[1,2]{1,0:T(1,128)} %bitcast.1), custom_call_target="tpu_custom_call" | custom-call | tf_op jit(solution)/shard_map/pallas_call | solution.py:211
  19.0 1.5 %shard_map.60 = (bf16[2,1,1,128,128]{4,3,2,1,0:T(8,128)(2,1)}, f32[2,2]{1,0:T(2,128)}) custom-call(bf16[2,1,1,128,128]{4,3,2,1,0:T(8,128)(2,1)} %get-tuple-element.4.res_in, f32[2,2]{1,0:T(2,128)} %get-tuple-element.5.sub_in), custom_call_target="tpu_custom_call" | custom-call | tf_op jit(solution)/shard_map/pallas_call | solution.py:238

commit v4 on v3

--- a/solution.py
+++ b/solution.py
@@ -83,7 +83,11 @@
             device_id_type=MESH,
         )
 
-    each(sectors, lambda step: r_copy(step, r_slot).start(), 1)
+    def r_start(step):
+        turned = 1 + lax.rem(step - lax.rem(sec, 2), sectors - 1)
+        r_copy(turned, r_slot).start()
+
+    each(sectors, r_start, 1)
     each(terms, lambda step: l_copy(step).start(), 1)
 
     @pl.when(owner != term)

time: 20.7 us -> 20.3 us (0.981)
  Pallas kernels: 19.9 us -> 19.5 us
    pallas_call x1, Pallas kernels: 18.4 us -> 17.9 us  [local(): pl.pallas_call(functools.partial(kernel, sectors, terms), out_shape=made,...]
where the time goes in v4:
time: 20.3 us; the launch traced here: 20.1 us
  Pallas kernels  19.5 us (96%)
  between operations  0.64 us (3%)
    pallas_call x1, Pallas kernels, local(): pl.pallas_call(functools.partial(kernel, sectors, terms), out_shape=made,...  17.9 us
    pallas_call x1, Pallas kernels, local(): pl.pallas_call(hand_on, out_shape=made, in_specs=[hbm, hbm], out_specs=(h...  1.51 us

profile of v4, /device:TPU:0, one launch (start us, length us, event | category | flops | bytes accessed | tf_op | source)
XLA Modules:
  0.0 20.1 jit_solution(13389806856779189149)
XLA Ops:
  0.6 17.9 %shard_map.59 = (bf16[2,1,1,128,128]{4,3,2,1,0:T(8,128)(2,1)}, f32[2,2]{1,0:T(2,128)}) custom-call(bf16[2,1,4,128,128]{4,3,2,1,0:T(8,128)(2,1)} %x_hbm.1, bf16[2,1,128,128]{3,2,1,0:T(8,128)(2,1)} %l_hbm.1, bf16[2,1,128,128]{3,2,1,0:T(8,128)(2,1)} %r_hbm.1, s32[1,2]{1,0:T(1,128)} %bitcast.1), custom_call_target="tpu_custom_call" | custom-call | tf_op jit(solution)/shard_map/pallas_call | solution.py:215
  18.6 1.5 %shard_map.60 = (bf16[2,1,1,128,128]{4,3,2,1,0:T(8,128)(2,1)}, f32[2,2]{1,0:T(2,128)}) custom-call(bf16[2,1,1,128,128]{4,3,2,1,0:T(8,128)(2,1)} %get-tuple-element.4.res_in, f32[2,2]{1,0:T(2,128)} %get-tuple-element.5.sub_in), custom_call_target="tpu_custom_call" | custom-call | tf_op jit(solution)/shard_map/pallas_call | solution.py:242
